TPU v7x, 32 devices: a whole 2x2x4 slice. The times are simulated.
32 devices in a mesh: gx: 8 (over z, x), gz: 4 (over y, core).
Axes of the slice: x: 2, y: 2, z: 4, core: 2. Of those that a mesh axis runs over, the one named last changes fastest.
Arguments:
- fields: float32 [3, 4096, 12288], P(None, 'gx', 'gz'), may hold values from -6 to 6
- register: float32 [3, 4096, 12288], P(None, 'gx', 'gz'), may hold values from -3 to 3
- source: float32 [4096, 12288], P('gx', 'gz'), may hold values from -0.25 to 0.25
- metric: float32 [4096], P('gx'), may hold values from 0.5 to 2
- curvature: float32 [4096], P('gx'), may hold values from -12 to 12
Outputs:
- new_fields: float32 [3, 4096, 12288], P(None, 'gx', 'gz')
- new_register: float32 [3, 4096, 12288], P(None, 'gx', 'gz')
- velocity: float32 [4096, 12288], P('gx', 'gz')
All inputs are finite; a program needn't handle non-finite values. Where the computation divides by a largest or mean magnitude, that divisor is 1e-20 or more.
Results may differ from a plain program's by a relative error of at most 0.0001.
Values sent between devices are 32-bit elements; how exact they have to be, the bound alone decides.
A program may use at most 320 MiB of HBM per device.

v0:
```python
import math

import jax
import jax.numpy as jnp
import numpy as np
from jax import lax
from jax.sharding import PartitionSpec as P

ALPHA_ONE = 1.0 / 3.0
COEF_ONE = 14.0 / 9.0
WIDE_ONE = 1.0 / 9.0
ALPHA_TWO = 2.0 / 11.0
COEF_TWO = 12.0 / 11.0
WIDE_TWO = 3.0 / 11.0
VISCOSITY = 0.25
DIFFUSIVITY = 0.2
COURANT = 1.2
KEEP_FACTOR = -5.0 / 9.0
STEP_FACTOR = 15.0 / 16.0


def with_halo(block, sides, width):
    for axis, dim in sides:
        count = lax.axis_size(axis)
        forward = [(i, i + 1) for i in range(count - 1)]
        backward = [(target, source) for source, target in forward]
        low = lax.ppermute(
            lax.slice_in_dim(block, block.shape[dim] - width, None, axis=dim), axis, forward
        )
        high = lax.ppermute(lax.slice_in_dim(block, 0, width, axis=dim), axis, backward)
        block = jnp.concatenate([low, block, high], axis=dim)
    return block


def shifted(value, axis, steps):
    count = lax.axis_size(axis)
    leading, last = (max(0, -steps), min(count, count - steps))
    return lax.ppermute(value, axis, [(source, source + steps) for source in range(leading, last)])


def log_sinh(values):
    return values + np.log(1.0 - np.exp(-2.0 * values)) - math.log(2.0)


def inverse_table(alpha, length):
    ratio = 0.5 / alpha
    angle_value = math.log(ratio + math.sqrt(ratio * ratio - 1.0))
    row_index = np.arange(1, length + 1) * 1.0
    smaller = np.minimum(row_index[:, None], row_index[None, :])
    larger = np.maximum(row_index[:, None], row_index[None, :])
    magnitude = (
        np.exp(
            log_sinh(smaller * angle_value)
            + log_sinh((length + 1 - larger) * angle_value)
            - log_sinh(angle_value)
            - log_sinh((length + 1) * angle_value)
        )
        / alpha
    )
    sign_table = np.where((row_index[:, None] + row_index[None, :]) % 2 == 0, 1.0, -1.0)
    return magnitude * sign_table


def first_right(padded):
    return COEF_ONE / 2.0 * (padded[:, 3:-1] - padded[:, 1:-3]) + WIDE_ONE / 4.0 * (
        padded[:, 4:] - padded[:, :-4]
    )


def second_right(padded):
    centre = padded[:, 2:-2]
    near = padded[:, 3:-1] - 2.0 * centre + padded[:, 1:-3]
    far = padded[:, 4:] - 2.0 * centre + padded[:, :-4]
    return COEF_TWO * near + WIDE_TWO / 4.0 * far


def local(fields, register, source, metric, curvature):
    group_size = lax.axis_size("gx")
    position = lax.axis_index("gx")
    cell_count = fields.shape[1]
    interior = cell_count - 1
    stretch = metric[:, None]
    curving = curvature[:, None]
    scaled_source = source / stretch
    wide_fields = with_halo(fields, (("gx", 1),), 2)
    lower_mask = jnp.asarray(np.tril(np.ones((cell_count, cell_count))), jnp.float32)
    running = jnp.dot(
        lower_mask,
        scaled_source,
        precision=lax.Precision.HIGHEST,
        preferred_element_type=jnp.float32,
    )
    totals = running[cell_count - 1 : cell_count]
    gathered = lax.all_gather(totals, "gx", axis=0, tiled=True)
    earlier = (jnp.arange(group_size) < position)[:, None]
    offset = jnp.sum(jnp.where(earlier, gathered, 0.0), axis=0, keepdims=True)
    velocity = -(offset + running - 0.5 * scaled_source)
    local_rate = jnp.max(jnp.abs(velocity) * stretch + 4.0 * VISCOSITY * stretch * stretch)
    max_rate = lax.pmax(local_rate, ("gx", "gz"))
    time_step = COURANT / max_rate
    wide_velocity = with_halo(velocity, (("gx", 0),), 2)
    first_sources = jnp.concatenate([wide_velocity[None], wide_fields], 0)
    right_one = first_right(first_sources)
    right_two = second_right(wide_fields)
    table_one = inverse_table(ALPHA_ONE, interior)
    table_two = inverse_table(ALPHA_TWO, interior)
    inner_one = jnp.einsum(
        "ij,sjl->sil",
        jnp.asarray(table_one, jnp.float32),
        right_one[:, :interior],
        precision=lax.Precision.HIGHEST,
        preferred_element_type=jnp.float32,
    )
    inner_two = jnp.einsum(
        "ij,sjl->sil",
        jnp.asarray(table_two, jnp.float32),
        right_two[:, :interior],
        precision=lax.Precision.HIGHEST,
        preferred_element_type=jnp.float32,
    )
    partial_rows = jnp.concatenate([inner_one, inner_two], 0)
    right_sides = jnp.concatenate([right_one, right_two], 0)
    alpha_rows = np.array([ALPHA_ONE] * 4 + [ALPHA_TWO] * 3)
    tables = [table_one] * 4 + [table_two] * 3
    left_cols = np.stack([-alpha_rows[k] * tables[k][:, 0] for k in range(7)])
    right_cols = np.stack([-alpha_rows[k] * tables[k][:, interior - 1] for k in range(7)])
    middle_denominator = (
        1.0 + alpha_rows * right_cols[:, interior - 1] + alpha_rows * left_cols[:, 0]
    )
    end_denominator = 1.0 + alpha_rows * right_cols[:, interior - 1]
    alpha_column = jnp.asarray(alpha_rows, jnp.float32)[:, None]
    middle_column = jnp.asarray(middle_denominator, jnp.float32)[:, None]
    end_column = jnp.asarray(end_denominator, jnp.float32)[:, None]
    first_rows = partial_rows[:, 0]
    last_rows = partial_rows[:, interior - 1]
    edge_rows = right_sides[:, cell_count - 1]
    next_first = shifted(first_rows, "gx", -1)
    denominator = jnp.where(position == group_size - 1, end_column, middle_column)
    own_separator = (edge_rows - alpha_column * last_rows - alpha_column * next_first) / denominator
    left_separator = shifted(own_separator, "gx", 1)
    left_table = jnp.asarray(left_cols, jnp.float32)[:, :, None]
    right_table = jnp.asarray(right_cols, jnp.float32)[:, :, None]
    inner_rows = (
        partial_rows
        + left_separator[:, None, :] * left_table
        + own_separator[:, None, :] * right_table
    )
    solutions = jnp.concatenate([inner_rows, own_separator[:, None, :]], 1)
    velocity_x = stretch * solutions[0]
    field_slope = solutions[1:4]
    field_bend = solutions[4:7]
    field_x = stretch * field_slope
    field_xx = stretch * stretch * field_bend + curving * field_slope
    diffusion = jnp.asarray(np.array([VISCOSITY, VISCOSITY, DIFFUSIVITY]), jnp.float32)[
        :, None, None
    ]
    tendency = -(velocity * field_x + fields * velocity_x) + diffusion * field_xx
    new_register = KEEP_FACTOR * register + time_step * tendency
    new_fields = fields + STEP_FACTOR * new_register
    return (new_fields, new_register, velocity)


def solution(mesh):
    placed = (P(None, "gx", "gz"), P(None, "gx", "gz"), P("gx", "gz"), P("gx"), P("gx"))
    return jax.shard_map(
        local,
        mesh=mesh,
        in_specs=placed,
        out_specs=(P(None, "gx", "gz"), P(None, "gx", "gz"), P("gx", "gz")),
        check_vma=False,
    )
```

profile of v0, /device:TPU:0, one launch (start us, length us, event | category | flops | bytes accessed | tf_op | source)
XLA Modules:
  0.0 635.3 jit_solution(14626419204117965836)
XLA Ops:
  0.6 0.0 copy-start.8
  0.6 0.8 mul.165
  1.4 13.4 %fusion.22 = f32[512,3072]{1,0:T(8,128)S(1)} fusion(f32[512,512]{1,0:T(8,128)} %constant.48.clone, f32[512,3072]{1,0:T(8,128)} %param.16, f32[512]{0:T(512)} %param.17), kind=kOutput, calls=%fused_computation.46 | convolution fusion | flops 9665249280 | bytes 13633536 | tf_op jit(solution)/shard_map/dot_general | solution.py:87
  14.9 0.0 copy-start.3
  14.9 2.7 copy-done.3
  17.6 32.3 %all-gather = f32[8,1,3072]{2,1,0:T(1,128)S(1)} all-gather(f32[1,1,3072]{2,1,0:T(1,128)S(1)} %slice_bitcast_fusion), channel_id=1, replica_groups=mesh['gx'=8,'gz'=4] {'gx'}, dimensions={0}, use_global_device_ids=true | all-gather | bytes 110592 | tf_op jit(solution)/shard_map/all_gather | solution.py:94
  49.9 0.1 fusion.29
  50.0 0.0 copy-done.8
  50.1 7.0 %add_reduce_fusion = (f32[]{:T(128)}, f32[512,3072]{1,0:T(8,128)S(1)}) fusion(f32[512]{0:T(512)S(1)} %mul.165, f32[512]{0:T(512)S(1)} %copy-done.8, f32[512,3072]{1,0:T(8,128)} %param.16, f32[512,3072]{1,0:T(8,128)} %copy-done.3, f32[3072]{0:T(1024)S(1)} %fusion.29), kind=kLoop, calls=%fused_computation.43 | loop fusion | flops 14155775 | bytes 18890756 | tf_op jit(solution)/shard_map/reduce_max | solution.py:98
  57.1 1.6 collective-permute-start.1
  58.6 4.9 collective-permute-start
  63.6 0.0 copy-done.1
  63.6 37.4 %copy.31 = f32[3,512,3072]{2,0,1:T(4,128)} copy(f32[3,512,3072]{2,1,0:T(8,128)S(1)} %copy-done.1) | data formatting | bytes 37748736 | tf_op args[0]
  101.0 0.0 copy-done.10
  101.0 0.0 copy-done.2
  101.0 1.0 fusion.32
  102.0 3.9 collective-permute-start.2
  105.9 1.5 collective-permute-start.3
  107.4 0.0 collective-permute-done.1
  107.4 0.0 collective-permute-done
  107.4 3.7 pad_maximum_fusion.2
  111.2 5.6 broadcast_in_dim.18
  116.8 0.0 collective-permute-done.2
  116.8 0.7 constant_dynamic-update-slice_fusion.1
  117.5 30.4 %copy_dynamic-update-slice_fusion.1 = (f32[3,514,3072]{2,0,1:T(4,128)}, f32[3,514,3072]{2,0,1:T(4,128)}) fusion(f32[3,512,3072]{2,1,0:T(8,128)} %param.14, f32[3,514,3072]{2,0,1:T(4,128)} %constant_dynamic-update-slice_fusion.1), kind=kLoop, calls=%fused_computation.48 | loop fusion | bytes 69206016
  147.9 0.0 collective-permute-done.3
  147.9 20.3 %maximum_maximum_fusion = f32[4,516,3072]{2,0,1:T(4,128)} fusion(f32[3,2,3072]{2,0,1:T(4,128)S(1)} %collective-permute-done.3, f32[3,512,3072]{2,0,1:T(4,128)} %copy.31, f32[3,2,3072]{2,0,1:T(4,128)S(1)} %collective-permute-done.2, f32[1,516,3072]{2,0,1:T(1,128)} %broadcast_in_dim.18), kind=kLoop, calls=%fused_computation.11 | loop fusion | flops 19021824 | bytes 50724864 | tf_op jit(solution)/shard_map/concatenate | solution.py:102
  168.2 41.4 %fusion.6 = f32[4,512,3072]{2,0,1:T(4,128)} fusion(f32[4,516,3072]{2,0,1:T(4,128)} %maximum_maximum_fusion), kind=kLoop, calls=%fused_computation.21 | loop fusion | flops 31457280 | bytes 125829120 | tf_op jit(solution)/shard_map/add | solution.py:65
  209.5 0.7 constant_dynamic-update-slice_fusion
  210.2 47.3 %fusion.3 = f32[3,512,3072]{2,0,1:T(4,128)} fusion(f32[3,514,3072]{2,0,1:T(4,128)} %get-tuple-element.16, f32[3,514,3072]{2,0,1:T(4,128)} %constant_dynamic-update-slice_fusion, f32[3,512,3072]{2,1,0:T(8,128)} %param.14), kind=kLoop, calls=%fused_computation.14 | loop fusion | flops 37748736 | bytes 113246208 | tf_op jit(solution)/shard_map/add | solution.py:74
  257.5 8.1 %slice-done = f32[3,511,3072]{2,0,1:T(4,128)S(1)} async-done(((f32[3,512,3072]{2,0,1:T(4,128)}), f32[3,511,3072]{2,0,1:T(4,128)S(1)}, s32[]{:S(2)}) %slice-start) | async-done | bytes 18837528 | tf_op jit(solution)/shard_map/slice | solution.py:117
  265.7 0.2 copy-done.4
  265.9 48.1 %fusion.17 = f32[3,3072,511]{1,2,0:T(8,128)} fusion(f32[511,511,1]{1,0,2:T(8,128)S(1)} %copy-done.4, f32[3,511,3072]{2,0,1:T(4,128)S(1)} %slice-done), kind=kOutput, calls=%fused_computation.36 | convolution fusion | flops 28877893632 | bytes 38719492 | tf_op jit(solution)/shard_map/ij,sjl->sil/dot_general | solution.py:114
  314.0 24.3 %copy.53 = f32[3,3072,511]{1,0,2:T(4,128)S(1)} copy(f32[3,3072,511]{1,2,0:T(8,128)} %fusion.17) | data formatting | bytes 37675008 | tf_op jit(solution)/shard_map/ij,sjl->sil/dot_general | solution.py:114
  338.3 0.0 copy-start
  338.3 0.0 copy-start.5
  338.3 27.4 %slice.97 = f32[4,511,3072]{2,0,1:T(4,128)} slice(f32[4,512,3072]{2,0,1:T(4,128)} %fusion.6), slice={[0:4], [0:511], [0:3072]} | slice | bytes 50233344 | tf_op jit(solution)/shard_map/slice | solution.py:110
  365.7 0.0 copy-done.5
  365.7 60.9 %fusion.8 = f32[4,3072,511]{1,2,0:T(8,128)} fusion(f32[511,511,1]{1,0,2:T(8,128)S(1)} %copy-done.5, f32[4,511,3072]{2,0,1:T(4,128)} %slice.97), kind=kOutput, calls=%fused_computation.24 | convolution fusion | flops 38503858176 | bytes 51277828 | tf_op jit(solution)/shard_map/ij,sjl->sil/dot_general | solution.py:107
  426.6 30.1 %copy.54 = f32[4,3072,511]{1,0,2:T(4,128)} copy(f32[4,3072,511]{1,2,0:T(8,128)} %fusion.8) | data formatting | bytes 50233344 | tf_op jit(solution)/shard_map/ij,sjl->sil/dot_general | solution.py:107
  456.7 0.9 fusion.30
  457.6 1.3 collective-permute-start.4
  458.9 0.0 copy-done.13
  458.9 0.0 copy-done.14
  458.9 0.0 copy-start.6
  458.9 0.0 copy-start.7
  458.9 5.8 collective-permute-done.4
  464.7 0.0 copy-done
  464.7 0.0 copy-done.16
  464.7 0.9 fusion.28
  465.6 4.8 collective-permute-start.5
  470.5 38.9 %pmax.7 = f32[]{:T(128)} all-reduce(f32[]{:T(128)} %get-tuple-element.11), channel_id=1, replica_groups=mesh['gx'=8,'gz'=4] {'gx','gz'}, use_global_device_ids=true, to_apply=%region_2.3 | all-reduce | flops 1 | bytes 8 | tf_op jit(solution)/shard_map/pmax | solution.py:99
  510.0 0.1 broadcast_in_dim.19
  510.1 0.0 collective-permute-done.5
  510.1 0.0 copy-done.6
  510.1 0.0 copy-done.7
  510.1 34.0 %fusion.1 = f32[7,511,3072]{2,0,1:T(8,128)} fusion(f32[3,511,3072]{2,0,1:T(4,128)} %bitcast.35, f32[4,511,3072]{2,0,1:T(4,128)} %bitcast.38, f32[7,511]{0,1:T(8,128)S(1)} %copy-done.6, f32[7,3072]{1,0:T(8,128)S(1)} %fusion.28, f32[7,511]{0,1:T(8,128)S(1)} %copy-done.7, f32[7,3072]{1,0:T(8,128)S(1)} %collective-permute-done.5), kind=kLoop, calls=%fused_computation.8 | loop fusion | flops 54942720 | bytes 88109000 | tf_op jit(solution)/shard_map/add | solution.py:144
  544.1 39.4 %copy.41 = f32[7,511,3072]{2,1,0:T(8,128)} copy(f32[7,511,3072]{2,0,1:T(8,128)} %fusion.1) | data formatting | bytes 87908352 | tf_op jit(solution)/shard_map/add | solution.py:144
  583.5 0.0 copy-done.9
  583.5 0.0 copy-start.12
  583.5 0.0 copy-start.15
  583.5 6.2 fusion.21
  589.7 0.0 copy-done.11
  589.7 45.2 %multiply_add_fusion = (f32[3,512,3072]{2,1,0:T(8,128)}, f32[3,512,3072]{2,1,0:T(8,128)}) fusion(f32[3,512,3072]{2,1,0:T(8,128)} %param.14, f32[512]{0:T(512)S(1)} %copy-done.12, f32[7,1,3072]{2,1,0:T(1,128)S(1)} %broadcast_in_dim.19, f32[7,511,3072]{2,1,0:T(8,128)} %copy.41, f32[512]{0:T(512)S(1)} %copy-done.11, f32[3]{0:T(128)S(1)} %copy-done.15, ...), kind=kLoop, calls=%fused_computation.38 | loop fusion | flops 80216064 | bytes 132126736 | tf_op jit(solution)/shard_map/add | solution.py:159
  (16 shorter events, 0.1 us)
Async XLA Ops:
  0.6 49.4 %copy-start.8 = (f32[512]{0:T(512)S(1)}, f32[512]{0:T(512)}, u32[]{:S(2)}) copy-start(f32[512]{0:T(512)} %param.17) | copy-start | bytes 6148
  1.4 99.6 %copy-start.10 = (f32[512]{0:T(512)}, f32[512]{0:T(512)S(1)}, u32[]{:S(2)}) copy-start(f32[512]{0:T(512)S(1)} %mul.165) | copy-start | bytes 6148
  14.9 2.7 copy-start.3
  49.9 13.6 %copy-start.1 = (f32[3,512,3072]{2,1,0:T(8,128)S(1)}, f32[3,512,3072]{2,1,0:T(8,128)}, u32[]{:S(2)}) copy-start(f32[3,512,3072]{2,1,0:T(8,128)} %param.14) | copy-start | bytes 56623108
  57.0 44.0 %copy-start.2 = (f32[512,3072]{1,0:T(8,128)}, f32[512,3072]{1,0:T(8,128)S(1)}, u32[]{:S(2)}) copy-start(f32[512,3072]{1,0:T(8,128)S(1)} %get-tuple-element.12) | copy-start | bytes 18874372
  57.1 50.3 %collective-permute-start.1 = (f32[2,3072]{1,0:T(2,128)S(1)}, f32[2,3072]{1,0:T(2,128)S(1)}, u32[]{:S(2)}, u32[]{:S(2)}) collective-permute-start(f32[2,3072]{1,0:T(2,128)S(1)} %get-tuple-element.18), channel_id=1, source_target_pairs={{4,0},{8,4},{12,8},{16,12},{20,16},{24,20},{28,24},{5,1},{9,5},{13... | collective-permute-start | bytes 73736 | tf_op jit(solution)/shard_map/ppermute | solution.py:30
  58.6 48.8 %collective-permute-start = (f32[2,3072]{1,0:T(2,128)S(1)}, f32[2,3072]{1,0:T(2,128)S(1)}, u32[]{:S(2)}, u32[]{:S(2)}) collective-permute-start(f32[2,3072]{1,0:T(2,128)S(1)} %get-tuple-element.17), channel_id=1, source_target_pairs={{0,4},{4,8},{8,12},{12,16},{16,20},{20,24},{24,28},{1,5},{5,9},{9,... | collective-permute-start | bytes 73736 | tf_op jit(solution)/shard_map/ppermute | solution.py:27
  102.0 14.8 %collective-permute-start.2 = (f32[3,2,3072]{2,0,1:T(4,128)S(1)}, f32[3,2,3072]{2,0,1:T(4,128)S(1)}, u32[]{:S(2)}, u32[]{:S(2)}) collective-permute-start(f32[3,2,3072]{2,0,1:T(4,128)S(1)} %get-tuple-element.14), channel_id=1, source_target_pairs={{0,4},{4,8},{8,12},{12,16},{16,20},{20,24},{24,28},{1,5},{5,9},{9,... | collective-permute-start | bytes 221192 | tf_op jit(solution)/shard_map/ppermute | solution.py:27
  105.9 42.0 %collective-permute-start.3 = (f32[3,2,3072]{2,0,1:T(4,128)S(1)}, f32[3,2,3072]{2,0,1:T(4,128)S(1)}, u32[]{:S(2)}, u32[]{:S(2)}) collective-permute-start(f32[3,2,3072]{2,0,1:T(4,128)S(1)} %get-tuple-element.13), channel_id=1, source_target_pairs={{4,0},{8,4},{12,8},{16,12},{20,16},{24,20},{28,24},{5,1},{9,5},{13... | collective-permute-start | bytes 221192 | tf_op jit(solution)/shard_map/ppermute | solution.py:30
  257.5 8.1 %slice-start = ((f32[3,512,3072]{2,0,1:T(4,128)}), f32[3,511,3072]{2,0,1:T(4,128)S(1)}, s32[]{:S(2)}) async-start(f32[3,512,3072]{2,0,1:T(4,128)} %fusion.3), calls=%async_computation | async-start | bytes 50233344 | tf_op jit(solution)/shard_map/slice | solution.py:117
  257.5 8.4 %copy-start.4 = (f32[511,511,1]{1,0,2:T(8,128)S(1)}, f32[511,511,1]{1,0,2:T(8,128)}, u32[]{:S(2)}) copy-start(f32[511,511,1]{1,0,2:T(8,128)} %constant.58) | copy-start | bytes 3133456
  338.3 126.4 %copy-start = (f32[3,3072,511]{1,0,2:T(4,128)}, f32[3,3072,511]{1,0,2:T(4,128)S(1)}, u32[]{:S(2)}) copy-start(f32[3,3072,511]{1,0,2:T(4,128)S(1)} %copy.53) | copy-start | bytes 56512516
  338.3 27.4 %copy-start.5 = (f32[511,511,1]{1,0,2:T(8,128)S(1)}, f32[511,511,1]{1,0,2:T(8,128)}, u32[]{:S(2)}) copy-start(f32[511,511,1]{1,0,2:T(8,128)} %constant.57) | copy-start | bytes 3133456
  456.7 2.2 copy-start.13
  456.7 2.2 copy-start.14
  456.7 8.0 %copy-start.16 = (f32[7]{0:T(128)S(1)}, f32[7]{0:T(128)}, u32[]{:S(2)}) copy-start(f32[7]{0:T(128)} %constant.51.clone) | copy-start | bytes 88
  457.6 7.1 %collective-permute-start.4 = (f32[7,3072]{1,0:T(8,128)S(1)}, f32[7,3072]{1,0:T(8,128)S(1)}, u32[]{:S(2)}, u32[]{:S(2)}) collective-permute-start(f32[7,3072]{1,0:T(8,128)S(1)} %fusion.30), channel_id=1, source_target_pairs={{4,0},{8,4},{12,8},{16,12},{20,16},{24,20},{28,24},{5,1},{9,5},{13... | collective-permute-start | bytes 258056 | tf_op jit(solution)/shard_map/ppermute | solution.py:38
  458.9 51.2 %copy-start.6 = (f32[7,511]{0,1:T(8,128)S(1)}, f32[7,511]{0,1:T(8,128)}, u32[]{:S(2)}) copy-start(f32[7,511]{0,1:T(8,128)} %constant.55.clone) | copy-start | bytes 42928
  458.9 51.2 %copy-start.7 = (f32[7,511]{0,1:T(8,128)S(1)}, f32[7,511]{0,1:T(8,128)}, u32[]{:S(2)}) copy-start(f32[7,511]{0,1:T(8,128)} %constant.54.clone) | copy-start | bytes 42928
  465.6 44.5 %collective-permute-start.5 = (f32[7,3072]{1,0:T(8,128)S(1)}, f32[7,3072]{1,0:T(8,128)S(1)}, u32[]{:S(2)}, u32[]{:S(2)}) collective-permute-start(f32[7,3072]{1,0:T(8,128)S(1)} %fusion.28), channel_id=1, source_target_pairs={{0,4},{4,8},{8,12},{12,16},{16,20},{20,24},{24,28},{1,5},{5,9},{9,... | collective-permute-start | bytes 258056 | tf_op jit(solution)/shard_map/ppermute | solution.py:38
  544.1 39.4 %copy-start.9 = (f32[512]{0:T(512)S(1)}, f32[512]{0:T(512)}, u32[]{:S(2)}) copy-start(f32[512]{0:T(512)} %param.17) | copy-start | bytes 6148
  583.5 6.2 copy-start.11
  583.5 6.2 copy-start.12
  583.5 6.2 copy-start.15
where the time goes:
time: 644 us; the launch traced here: 635 us
  local copies, waits for them, and re-layouts  208 us (32%)
  other arithmetic  208 us (32%)
  matrix products  122 us (19%)
  blocking collectives  71.2 us (11%)
  starting transfers between devices  18 us (3%)
    unnamed x38, local copies, waits for them, and re-layouts  71.5 us
    dot_general x1, matrix products, local(): jnp.einsum('ij,sjl->sil', jnp.asarray(table_one, jnp.float32), right_one[...  60.9 us
    dot_general x1, matrix products, local(): jnp.einsum('ij,sjl->sil', jnp.asarray(table_two, jnp.float32), right_two[...  48.1 us
    add x1, other arithmetic, second_right(): return COEF_TWO * near + WIDE_TWO / 4.0 * far  47.3 us
    add x1, other arithmetic, local(): new_fields = fields + STEP_FACTOR * new_register  45.2 us
    add x1, other arithmetic, first_right(): COEF_ONE / 2.0 * (padded[:, 3:-1] - padded[:, 1:-3])  41.4 us
    add x1, local copies, waits for them, and re-layouts, local(): partial_rows + left_separator[:, None, :] * left_table  39.4 us
    pmax x1, blocking collectives, local(): max_rate = lax.pmax(local_rate, ('gx', 'gz'))  38.9 us
  transfers between devices with their start and end apart: 6, of which 1 were waited for; matrix products, arithmetic and copies ran while one was open for 12% of the time, Pallas kernels for 0%

commit v1 on v0

v1 whole, which is shorter than its diff:
```python
import functools
import math

import jax
import jax.numpy as jnp
import numpy as np
from jax import lax
from jax.experimental import pallas as pl
from jax.experimental.pallas import tpu as pltpu
from jax.sharding import PartitionSpec as P

ALPHA_ONE = 1.0 / 3.0
COEF_ONE = 14.0 / 9.0
WIDE_ONE = 1.0 / 9.0
ALPHA_TWO = 2.0 / 11.0
COEF_TWO = 12.0 / 11.0
WIDE_TWO = 3.0 / 11.0
VISCOSITY = 0.25
DIFFUSIVITY = 0.2
DIFFUSIONS = (VISCOSITY, VISCOSITY, DIFFUSIVITY)
COURANT = 1.2
KEEP_FACTOR = -5.0 / 9.0
STEP_FACTOR = 15.0 / 16.0

MESH = pl.DeviceIdType.MESH
LANES = 128
LOADS = 4
SYSTEMS = 7

NEAR_ONE, FAR_ONE = COEF_ONE / 2.0, WIDE_ONE / 4.0
NEAR_TWO, FAR_TWO = COEF_TWO, WIDE_TWO / 4.0
STENCIL_ONE = (-FAR_ONE, -NEAR_ONE, 0.0, NEAR_ONE, FAR_ONE)
STENCIL_TWO = (FAR_TWO, NEAR_TWO, -2.0 * (NEAR_TWO + FAR_TWO), NEAR_TWO, FAR_TWO)
STENCIL_SUM = (
    -0.5 * FAR_ONE,
    -(0.5 * NEAR_ONE + FAR_ONE),
    -(NEAR_ONE + FAR_ONE),
    -(0.5 * NEAR_ONE + FAR_ONE),
    -0.5 * FAR_ONE,
)


def log_sinh(values):
    return values + np.log(1.0 - np.exp(-2.0 * values)) - math.log(2.0)


def inverse_table(alpha, length):
    ratio = 0.5 / alpha
    angle_value = math.log(ratio + math.sqrt(ratio * ratio - 1.0))
    row_index = np.arange(1, length + 1) * 1.0
    smaller = np.minimum(row_index[:, None], row_index[None, :])
    larger = np.maximum(row_index[:, None], row_index[None, :])
    magnitude = (
        np.exp(
            log_sinh(smaller * angle_value)
            + log_sinh((length + 1 - larger) * angle_value)
            - log_sinh(angle_value)
            - log_sinh((length + 1) * angle_value)
        )
        / alpha
    )
    sign_table = np.where((row_index[:, None] + row_index[None, :]) % 2 == 0, 1.0, -1.0)
    return magnitude * sign_table


def stencil_table(stencil, length):
    return sum(stencil[k + 2] * np.eye(length, k=k) for k in range(-2, 3))


def wide(table):
    return np.repeat(np.asarray(table, np.float32)[..., None], LANES, axis=-1)


def reach_of(column):
    kept = int(np.max(np.nonzero(np.asarray(column, np.float32))[0])) + 1
    return min(len(column), -(-kept // 16) * 16)


@functools.lru_cache(maxsize=None)
def tables(block):
    inv_one, inv_two = inverse_table(ALPHA_ONE, block), inverse_table(ALPHA_TWO, block)
    maps = (
        inv_one @ stencil_table(STENCIL_SUM, block),
        inv_one @ stencil_table(STENCIL_ONE, block),
        inv_two @ stencil_table(STENCIL_TWO, block),
    )
    reach = (reach_of(inv_one[:, 0]), reach_of(inv_two[:, 0]))
    columns = np.stack([inv_one[:, 0], inv_one[:, -1], inv_two[:, 0], inv_two[:, -1]])
    edge = max(reach_of(maps[k][0]) for k in range(3))
    firsts = np.stack([maps[k][0, :edge] for k in range(3)])
    lasts = np.stack([maps[k][-1, block - edge :] for k in range(3)])
    alphas = [ALPHA_ONE] * 4 + [ALPHA_TWO] * 3
    stencils = [STENCIL_SUM] + [STENCIL_ONE] * 3 + [STENCIL_TWO] * 3
    taus = [inv_one[0, 0]] * 4 + [inv_two[0, 0]] * 3
    joins = np.zeros((9, 8))
    for s in range(SYSTEMS):
        kappa = taus[s] * alphas[s]
        joins[:, s] = (
            stencils[s][3], stencils[s][4], stencils[s][1], stencils[s][0],
            1.0 / alphas[s], alphas[s], taus[s], kappa, 1.0 / (1.0 - kappa * kappa),
        )
    return dict(
        maps=np.stack(maps).astype(np.float32),
        reach=reach, columns=wide(columns), edge=edge, firsts=wide(firsts), lasts=wide(lasts),
        joins=wide(joins),
    )


def two_parts(values):
    high = values.astype(jnp.bfloat16)
    low = (values - high.astype(jnp.float32)).astype(jnp.bfloat16)
    return high, low


def lower_mask(block):
    rows = lax.broadcasted_iota(jnp.int32, (block, block), 0)
    columns = lax.broadcasted_iota(jnp.int32, (block, block), 1)
    return jnp.where(columns <= rows, 1.0, 0.0).astype(jnp.bfloat16)


def fill_column(column_ref, row_ref, change=lambda values: values):
    cells = row_ref.shape[1]
    size = min(LANES, cells)
    for r in range(0, cells, size):
        square = jnp.broadcast_to(row_ref[0:1, r : r + size], (LANES, size))
        column_ref[r : r + size] = change(jnp.transpose(square))


def spread(table, lanes):
    return jnp.concatenate([table] * (lanes // LANES), axis=-1) if lanes > LANES else table


def talk_kernel(
    group, bundles, block, edge, chunk,
    fields_ref, source_ref, metric_row_ref, firsts_ref, lasts_ref,
    halo_ref, offset_ref, step_ref,
    metric_ref, inverse_ref, mask_ref, src, run, tops, ends, totals, total_in, edges, halo, rate, rate_in, rate_two, rate_two_in,
    load_sem, tot_send, tot_recv, edge_send, edge_recv, one_send, one_recv, two_send, two_recv,
):
    cells, lines = src.shape
    parts = cells // block
    here, bundle = lax.axis_index("gx"), lax.axis_index("gz")
    pieces = lines // chunk
    broad = 512 if lines % 512 == 0 else chunk

    share = cells // LOADS
    loads = []
    for k in range(LOADS):
        rows = pl.ds(k * share, share)
        loads.append(pltpu.make_async_copy(source_ref.at[rows], src.at[rows], load_sem.at[k]))
    top_load = pltpu.make_async_copy(fields_ref.at[:, pl.ds(0, edge)], tops, load_sem.at[LOADS])
    end_load = pltpu.make_async_copy(fields_ref.at[:, pl.ds(cells - edge, edge)], ends, load_sem.at[LOADS + 1])
    for load in loads + [top_load, end_load]:
        load.start()

    barrier = pltpu.get_barrier_semaphore()

    def along(d):
        return (lax.rem(here + d, group), bundle)

    def across(d):
        return (here, lax.rem(bundle + d, bundles))

    @pl.loop(1, group)
    def _(d):
        pl.semaphore_signal(barrier, inc=1, device_id=along(d), device_id_type=MESH)

    @pl.loop(1, bundles)
    def _(d):
        pl.semaphore_signal(barrier, inc=1, device_id=across(d), device_id_type=MESH)

    fill_column(metric_ref, metric_row_ref)
    fill_column(inverse_ref, metric_row_ref, lambda values: 1.0 / values)
    mask = lower_mask(block)
    mask_ref[:, :block] = mask
    mask_ref[:, block:] = mask

    for k in range(LOADS):
        loads[k].wait()

        @pl.loop(0, lines // broad)
        def _(j):
            at = pl.ds(pl.multiple_of(j * broad, broad), broad)
            acc = jnp.zeros((8, broad), jnp.float32)
            for r in range(k * share, (k + 1) * share, 8):
                scaled = src[r : r + 8, at] * spread(inverse_ref[r : r + 8], broad)
                src[r : r + 8, at] = scaled
                acc = acc + scaled
            total = jnp.sum(acc, axis=0, keepdims=True)
            totals[0:1, at] = total if k == 0 else totals[0:1, at] + total

    pl.semaphore_wait(barrier, group + bundles - 2)

    def total_copy(d):
        return pltpu.make_async_remote_copy(
            src_ref=totals, dst_ref=total_in.at[d], send_sem=tot_send.at[d], recv_sem=tot_recv.at[d],
            device_id=along(d), device_id_type=MESH,
        )

    @pl.loop(1, group)
    def _(d):
        total_copy(d).start()

    top_load.wait()
    end_load.wait()

    edges[0, 7:8, :] = jnp.zeros((1, lines), jnp.float32)
    edges[1, 7:8, :] = jnp.zeros((1, lines), jnp.float32)

    @pl.loop(0, pieces)
    def _(j):
        at = pl.ds(pl.multiple_of(j * chunk, chunk), chunk)
        for side, weights in ((0, lasts_ref), (1, firsts_ref)):
            base = cells - edge if side == 0 else 0
            acc = jnp.zeros((8, chunk), jnp.float32)
            for r in range(0, edge, 8):
                acc = acc + src[base + r : base + r + 8, at] * spread(weights[0, r : r + 8], chunk)
            edges[side, 0:1, at] = jnp.sum(acc, axis=0, keepdims=True)
            outer = cells - 1 if side == 0 else 0
            inner = cells - 2 if side == 0 else 1
            edges[side, 8:9, at] = src[outer : outer + 1, at]
            edges[side, 12:13, at] = src[inner : inner + 1, at]
            rows = ends if side == 0 else tops
            for c in range(3):
                one = jnp.zeros((8, chunk), jnp.float32)
                two = jnp.zeros((8, chunk), jnp.float32)
                for r in range(0, edge, 8):
                    value = rows[c, r : r + 8, at]
                    one = one + value * spread(weights[1, r : r + 8], chunk)
                    two = two + value * spread(weights[2, r : r + 8], chunk)
                edges[side, 1 + c : 2 + c, at] = jnp.sum(one, axis=0, keepdims=True)
                edges[side, 4 + c : 5 + c, at] = jnp.sum(two, axis=0, keepdims=True)
                outer = edge - 1 if side == 0 else 0
                inner = edge - 2 if side == 0 else 1
                edges[side, 9 + c : 10 + c, at] = rows[c, outer : outer + 1, at]
                edges[side, 13 + c : 14 + c, at] = rows[c, inner : inner + 1, at]

    edge_copies = [
        pltpu.make_async_remote_copy(
            src_ref=edges.at[side], dst_ref=halo.at[side], send_sem=edge_send.at[side],
            recv_sem=edge_recv.at[side], device_id=along(1 if side == 0 else group - 1), device_id_type=MESH,
        )
        for side in range(2)
    ]
    for copy in edge_copies:
        copy.start()

    @pl.loop(0, pieces)
    def _(j):
        at = pl.ds(pl.multiple_of(j * chunk, chunk), chunk)
        before = jnp.zeros((1, chunk), jnp.float32)
        for k in range(parts):
            scaled = src[k * block : (k + 1) * block, at]
            high, low = two_parts(scaled)
            sums = jnp.dot(mask_ref[...], jnp.concatenate([high, low], axis=0), preferred_element_type=jnp.float32)
            run[k * block : (k + 1) * block, at] = before + sums - 0.5 * scaled
            before = before + sums[block - 1 : block]

    @pl.loop(1, group)
    def _(d):
        total_copy(d).wait()

    def earlier(d, acc):
        return acc + jnp.where(d <= here, total_in[d], 0.0)

    offset = lax.fori_loop(1, group, earlier, jnp.zeros((1, lines), jnp.float32))
    offset_ref[0:1, :] = offset
    offset_ref[1:8, :] = jnp.zeros((7, lines), jnp.float32)

    rate[...] = jnp.zeros((8, LANES), jnp.float32)

    @pl.loop(0, lines // broad)
    def _(j):
        at = pl.ds(pl.multiple_of(j * broad, broad), broad)
        before = offset_ref[0:1, at]
        acc = jnp.zeros((8, broad), jnp.float32)
        for r in range(0, cells, 8):
            stretch = spread(metric_ref[r : r + 8], broad)
            speed = jnp.abs(before + run[r : r + 8, at])
            acc = jnp.maximum(acc, speed * stretch + 4.0 * VISCOSITY * stretch * stretch)
        for k in range(broad // LANES):
            rate[...] = jnp.maximum(rate[...], acc[:, k * LANES : (k + 1) * LANES])

    def one_copy(d):
        return pltpu.make_async_remote_copy(
            src_ref=rate, dst_ref=rate_in.at[d], send_sem=one_send.at[d], recv_sem=one_recv.at[d],
            device_id=along(d), device_id_type=MESH,
        )

    def two_copy(d):
        return pltpu.make_async_remote_copy(
            src_ref=rate_two, dst_ref=rate_two_in.at[d], send_sem=two_send.at[d], recv_sem=two_recv.at[d],
            device_id=across(d), device_id_type=MESH,
        )

    @pl.loop(1, group)
    def _(d):
        one_copy(d).start()

    @pl.loop(1, group)
    def _(d):
        one_copy(d).wait()

    rate_two[...] = lax.fori_loop(1, group, lambda d, acc: jnp.maximum(acc, rate_in[d]), rate[...])

    @pl.loop(1, bundles)
    def _(d):
        two_copy(d).start()

    @pl.loop(1, bundles)
    def _(d):
        two_copy(d).wait()

    largest = lax.fori_loop(1, bundles, lambda d, acc: jnp.maximum(acc, rate_two_in[d]), rate_two[...])
    place = jnp.full((1, LANES), here, jnp.int32)
    step_ref[...] = COURANT / jnp.broadcast_to(jnp.max(largest), (8, LANES))
    step_ref[1:2, :] = jnp.where(place > 0, 1.0, 0.0)
    step_ref[2:3, :] = jnp.where(place < group - 1, 1.0, 0.0)

    for copy in edge_copies:
        copy.wait()
    halo_ref[...] = halo[...]


def talk(fields, source, metric, const, group, bundles, block):
    cells, lines = source.shape
    chunk = 256 if lines % 256 == 0 else LANES
    edge = const["edge"]
    parts = cells // block
    vmem, dma = pltpu.VMEM, pltpu.SemaphoreType.DMA
    f32 = jnp.float32
    whole = pl.BlockSpec(memory_space=pltpu.VMEM)
    held = pl.BlockSpec(memory_space=pl.ANY)
    return pl.pallas_call(
        functools.partial(talk_kernel, group, bundles, block, edge, chunk),
        out_shape=(
            jax.ShapeDtypeStruct((2, 16, lines), f32),
            jax.ShapeDtypeStruct((8, lines), f32),
            jax.ShapeDtypeStruct((8, LANES), f32),
        ),
        in_specs=[held, held] + [whole] * 3,
        out_specs=(whole,) * 3,
        scratch_shapes=[
            vmem((cells, LANES), f32), vmem((cells, LANES), f32), vmem((block, 2 * block), jnp.bfloat16),
            vmem((cells, lines), f32), vmem((cells, lines), f32),
            vmem((3, edge, lines), f32), vmem((3, edge, lines), f32),
            vmem((1, lines), f32), vmem((group, 1, lines), f32),
            vmem((2, 16, lines), f32), vmem((2, 16, lines), f32),
            vmem((8, LANES), f32), vmem((group, 8, LANES), f32),
            vmem((8, LANES), f32), vmem((bundles, 8, LANES), f32),
            dma((LOADS + 2,)), dma((group,)), dma((group,)), dma((2,)), dma((2,)),
            dma((group,)), dma((group,)), dma((bundles,)), dma((bundles,)),
        ],
        compiler_params=pltpu.CompilerParams(
            collective_id=0, has_side_effects=True, vmem_limit_bytes=48 * 2**20
        ),
        name="talk",
    )(
        fields, source, metric, jnp.asarray(const["firsts"]), jnp.asarray(const["lasts"]),
    )


def join(coef, last, outer_l, inner_l, first, outer_r, inner_r):
    rp1, rp2, rm1, rm2, over, alpha, tau, kappa, scale = coef
    edge_l = rp2 * outer_r * over
    edge_r = rm2 * outer_l * over
    near_l = rp1 * outer_r + rp2 * inner_r - edge_l
    near_r = rm1 * outer_l + rm2 * inner_l - edge_r
    a = last + tau * near_l + edge_l
    b = first + tau * near_r + edge_r
    first_x = (b - kappa * a) * scale
    last_x = (a - kappa * b) * scale
    return near_l - alpha * first_x, edge_l, near_r - alpha * last_x, edge_r


def main_kernel(
    block, reach, rows_at_once,
    step_ref, fields_ref, register_ref, source_ref, metric_row_ref, curving_row_ref,
    offset_ref, halo_ref, maps_ref, columns_ref, joins_ref,
    new_fields_ref, new_register_ref, velocity_ref,
    inverse_ref, metric_ref, curving_ref, source_map_ref, field_map_ref,
    solved, firsts, lasts, cells_at, add,
):
    cells, lines = source_ref.shape
    parts = cells // block
    f32 = jnp.float32

    @pl.when(pl.program_id(0) == 0)
    def _():
        fill_column(metric_ref, metric_row_ref)
        fill_column(inverse_ref, metric_row_ref, lambda values: 1.0 / values)
        fill_column(curving_ref, curving_row_ref)
        mask = lower_mask(block)
        source_map_ref[:block, :block] = mask
        source_map_ref[:block, block : 2 * block] = mask
        source_map_ref[:block, 2 * block :] = jnp.zeros((block, block), jnp.bfloat16)
        for m, (table, start) in enumerate(((source_map_ref, block), (field_map_ref, 0), (field_map_ref, block))):
            high, low = two_parts(maps_ref[m])
            table[start : start + block, :block] = high
            table[start : start + block, block : 2 * block] = high
            table[start : start + block, 2 * block :] = low

    for k in range(parts):
        rows = slice(k * block, (k + 1) * block)
        for c in range(4):
            if c == 0:
                value = source_ref[rows] * spread(inverse_ref[rows], lines)
                table = source_map_ref
            else:
                value = fields_ref[c - 1, rows]
                table = field_map_ref
            high, low = two_parts(value)
            solved[k, c] = jnp.dot(
                table[...], jnp.concatenate([high, low, high], axis=0), preferred_element_type=f32
            )
            for e, r in enumerate((0, 1, block - 1, block - 2)):
                row = value[r : r + 1]
                cells_at[k, e, c : c + 1] = row
                if c > 0:
                    cells_at[k, e, 3 + c : 4 + c] = row
        for into, r in ((firsts, 0), (lasts, block - 1)):
            into[k, 0:1] = solved[k, 0, block + r : block + r + 1]
            for c in range(3):
                into[k, 1 + c : 2 + c] = solved[k, 1 + c, r : r + 1]
                into[k, 4 + c : 5 + c] = solved[k, 1 + c, block + r : block + r + 1]
            into[k, 7:8] = jnp.zeros((1, lines), f32)
        for e in range(4):
            cells_at[k, e, 7:8] = jnp.zeros((1, lines), f32)

    coef = [spread(joins_ref[i], lines) for i in range(9)]
    before = [offset_ref[0:1, :]]
    for k in range(parts):
        before.append(before[-1] + solved[k, 0, block - 1 : block])

    def far_cells(side, start):
        own = halo_ref[side, start : start + 4]
        return jnp.concatenate([own, own[1:4], jnp.zeros((1, lines), f32)], axis=0)

    has_before, has_after = spread(step_ref[1:2], lines), spread(step_ref[2:3], lines)
    _, _, near, at_edge = join(
        coef, halo_ref[0, 0:8], far_cells(0, 8), far_cells(0, 12), firsts[0], cells_at[0, 0], cells_at[0, 1]
    )
    add[0, 0], add[0, 1] = near * has_before, at_edge * has_before
    for k in range(parts - 1):
        add[k, 2], add[k, 3], add[k + 1, 0], add[k + 1, 1] = join(
            coef, lasts[k], cells_at[k, 2], cells_at[k, 3],
            firsts[k + 1], cells_at[k + 1, 0], cells_at[k + 1, 1],
        )
    k = parts - 1
    near, at_edge, _, _ = join(
        coef, lasts[k], cells_at[k, 2], cells_at[k, 3], halo_ref[1, 0:8], far_cells(1, 8), far_cells(1, 12)
    )
    add[k, 2], add[k, 3] = near * has_after, at_edge * has_after
    beyond = before[parts] * (1.0 - has_after)
    add[k, 2, 0:1] = add[k, 2, 0:1] + (NEAR_ONE + FAR_ONE - FAR_ONE / ALPHA_ONE) * beyond
    add[k, 3, 0:1] = add[k, 3, 0:1] + (FAR_ONE / ALPHA_ONE) * beyond

    time_step = spread(step_ref[0:1], lines)
    for k in range(parts):
        places = [(0, block)] + [(1 + c, 0) for c in range(3)] + [(1 + c, block) for c in range(3)]
        for s, (slot, start) in enumerate(places):
            solved[k, slot, start : start + 1] += add[k, 1, s : s + 1]
            solved[k, slot, start + block - 1 : start + block] += add[k, 3, s : s + 1]

        for r in range(0, block, rows_at_once):
            rows = slice(k * block + r, k * block + r + rows_at_once)

            def whole(s):
                slot, start = places[s]
                kind = 0 if s < 4 else 1
                value = solved[k, slot, start + r : start + r + rows_at_once]
                if r < reach[kind]:
                    column = spread(columns_ref[2 * kind, r : r + rows_at_once], lines)
                    value = value + column * add[k, 0, s : s + 1]
                if r + rows_at_once > block - reach[kind]:
                    column = spread(columns_ref[2 * kind + 1, r : r + rows_at_once], lines)
                    value = value + column * add[k, 2, s : s + 1]
                return value

            stretch = spread(metric_ref[rows], lines)
            curving = spread(curving_ref[rows], lines)
            scaled = source_ref[rows] * spread(inverse_ref[rows], lines)
            velocity = 0.5 * scaled - (before[k] + solved[k, 0, r : r + rows_at_once])
            velocity_ref[rows] = velocity
            carried = velocity * stretch
            squeezed = (time_step * stretch) * whole(0)
            bent = time_step * stretch * stretch
            for c in range(3):
                on_slope = time_step * (DIFFUSIONS[c] * curving - carried)
                field = fields_ref[c, rows]
                change = on_slope * whole(1 + c) + (DIFFUSIONS[c] * bent) * whole(4 + c) - field * squeezed
                updated = KEEP_FACTOR * register_ref[c, rows] + change
                new_register_ref[c, rows] = updated
                new_fields_ref[c, rows] = field + STEP_FACTOR * updated


def compute(fields, register, source, metric, curving, halo, offset, step, const, block):
    cells, lines = source.shape
    width = 256 if lines % 256 == 0 else LANES
    parts = cells // block
    f32 = jnp.float32

    def fixed(array):
        rank = array.ndim
        return pl.BlockSpec(array.shape, lambda j: (0,) * rank)

    three = pl.BlockSpec((3, cells, width), lambda j: (0, 0, j))
    flat = pl.BlockSpec((cells, width), lambda j: (0, j))
    maps, columns, joins = jnp.asarray(const["maps"]), jnp.asarray(const["columns"]), jnp.asarray(const["joins"])
    return pl.pallas_call(
        functools.partial(main_kernel, block, const["reach"], min(32, block)),
        grid=(lines // width,),
        out_shape=(
            jax.ShapeDtypeStruct(fields.shape, f32),
            jax.ShapeDtypeStruct(register.shape, f32),
            jax.ShapeDtypeStruct(source.shape, f32),
        ),
        in_specs=[
            fixed(step), three, three, flat, fixed(metric), fixed(curving),
            pl.BlockSpec((8, width), lambda j: (0, j)),
            pl.BlockSpec((2, 16, width), lambda j: (0, 0, j)),
            fixed(maps), fixed(columns), fixed(joins),
        ],
        out_specs=(three, three, flat),
        scratch_shapes=[
            pltpu.VMEM((cells, LANES), f32), pltpu.VMEM((cells, LANES), f32), pltpu.VMEM((cells, LANES), f32),
            pltpu.VMEM((2 * block, 3 * block), jnp.bfloat16), pltpu.VMEM((2 * block, 3 * block), jnp.bfloat16),
            pltpu.VMEM((parts, 4, 2 * block, width), f32),
            pltpu.VMEM((parts, 8, width), f32),
            pltpu.VMEM((parts, 8, width), f32),
            pltpu.VMEM((parts, 4, 8, width), f32),
            pltpu.VMEM((parts, 4, 8, width), f32),
        ],
        compiler_params=pltpu.CompilerParams(vmem_limit_bytes=48 * 2**20),
        name="compute",
    )(
        step, fields, register, source, metric, curving, offset, halo, maps, columns, joins,
    )


def local(fields, register, source, metric, curvature):
    group, bundles = lax.axis_size("gx"), lax.axis_size("gz")
    cells = source.shape[0]
    block = min(256, cells)
    const = tables(block)
    metric_row, curving_row = metric.reshape(1, cells), curvature.reshape(1, cells)
    halo, offset, step = talk(fields, source, metric_row, const, group, bundles, block)
    return compute(fields, register, source, metric_row, curving_row, halo, offset, step, const, block)


def solution(mesh):
    placed = (P(None, "gx", "gz"), P(None, "gx", "gz"), P("gx", "gz"), P("gx"), P("gx"))
    return jax.shard_map(
        local,
        mesh=mesh,
        in_specs=placed,
        out_specs=(P(None, "gx", "gz"), P(None, "gx", "gz"), P("gx", "gz")),
        check_vma=False,
    )
```

time: 644 us -> 67.9 us (0.11); the launches traced: 635 us -> 67.7 us
  other arithmetic: 208 us -> 0 us
  local copies, waits for them, and re-layouts: 208 us -> 2.63 us
  matrix products: 122 us -> 0 us
  blocking collectives: 71.2 us -> 0 us
  Pallas kernels: 0 us -> 64.4 us
  starting transfers between devices: 18 us -> 0 us
    add x4 -> x0, other arithmetic: 168 us -> none  [the longest x1 47.3 us: second_right(): return COEF_TWO * near + WIDE_TWO / 4.0 * far]
    dot_general x3 -> x0, matrix products: 122 us -> none  [the longest x1 60.9 us: local(): jnp.einsum('ij,sjl->sil', jnp.asarray(table_one, jnp.float32), right_one[...]
    unnamed x38 -> x14, local copies, waits for them, and re-layouts: 71.5 us -> 2.63 us
    pallas_call x0 -> x2, Pallas kernels: none -> 64.4 us  [the longest x1 40.1 us: compute(): pl.pallas_call(functools.partial(main_kernel, block, const['reach'], min(...]
    dot_general x2 -> x0, local copies, waits for them, and re-layouts: 54.3 us -> none  [the longest x1 30.1 us: local(): jnp.einsum('ij,sjl->sil', jnp.asarray(table_one, jnp.float32), right_one[...]
    add x1 -> x0, local copies, waits for them, and re-layouts: 39.4 us -> none  [local(): partial_rows + left_separator[:, None, :] * left_table]
    pmax x1 -> x0, blocking collectives: 38.9 us -> none  [local(): max_rate = lax.pmax(local_rate, ('gx', 'gz'))]
    slice x5 -> x0, local copies, waits for them, and re-layouts: 36.6 us -> none  [the longest x1 27.4 us: local(): right_one[:, :interior]]
  transfers between devices with their start and end apart: 6 -> 0, of which waited for: 1 -> 0; matrix products, arithmetic and copies ran while one was open for 12% -> 0% of each run, Pallas kernels for 0% -> 0%
where the time goes in v1:
time: 67.9 us; the launch traced here: 67.7 us
  Pallas kernels  64.4 us (95%)
  local copies, waits for them, and re-layouts  2.63 us (4%)
  between operations  0.7 us (1%)
    pallas_call x1, Pallas kernels, compute(): pl.pallas_call(functools.partial(main_kernel, block, const['reach'], min(...  40.1 us
    pallas_call x1, Pallas kernels, talk(): pl.pallas_call(functools.partial(talk_kernel, group, bundles, block, edge...  24.2 us
    unnamed x14, local copies, waits for them, and re-layouts  2.63 us

profile of v1, /device:TPU:0, one launch (start us, length us, event | category | flops | bytes accessed | tf_op | source)
XLA Modules:
  0.0 67.7 jit_solution(15584413912045778704)
XLA Ops:
  0.6 0.0 copy-start.1
  0.6 0.0 copy-start
  0.7 0.0 copy-start.2
  0.7 1.0 %copy-done.2 = f32[3,112,128]{2,1,0:T(8,128)S(1)} copy-done((f32[3,112,128]{2,1,0:T(8,128)S(1)}, f32[3,112,128]{2,1,0:T(8,128)}, u32[]{:S(2)}) %copy-start.2) | copy-done | bytes 172056
  1.7 0.0 copy-start.3
  1.7 0.9 %copy-done.3 = f32[3,112,128]{2,1,0:T(8,128)S(1)} copy-done((f32[3,112,128]{2,1,0:T(8,128)S(1)}, f32[3,112,128]{2,1,0:T(8,128)}, u32[]{:S(2)}) %copy-start.3) | copy-done | bytes 172056
  2.6 0.0 copy-start.5
  2.6 0.7 %copy-done.5 = f32[512]{0:T(512)S(1)} copy-done((f32[512]{0:T(512)S(1)}, f32[512]{0:T(512)}, u32[]{:S(2)}) %copy-start.5) | copy-done | bytes 2072
  3.3 0.0 copy-start.4
  3.3 0.0 copy-start.6
  3.3 24.2 %talk.1 = (f32[2,16,3072]{2,1,0:T(8,128)S(1)}, f32[8,3072]{1,0:T(8,128)S(1)}, f32[8,128]{1,0:T(8,128)S(1)}) custom-call(f32[3,512,3072]{2,1,0:T(8,128)} %fields_ref.3, f32[512,3072]{1,0:T(8,128)} %source_ref.3, f32[1,512]{1,0:T(1,128)S(1)} %bitcast.2, f32[3,112,128]{2,1,0:T(8,128)S(1)} %copy-done.3, f32[3,112,128]{2,1,0:T(8,128)S(1)} %copy-done.2), custom_call_target="tpu_custom_call" | custom-call | tf_op jit(solution)/shard_map/talk/pallas_call | solution.py:334
  27.5 0.0 copy-done.1
  27.5 0.0 copy-done
  27.6 0.0 copy-done.4
  27.6 0.0 copy-done.6
  27.6 40.1 %compute.1 = (f32[3,512,3072]{2,1,0:T(8,128)}, f32[3,512,3072]{2,1,0:T(8,128)}, f32[512,3072]{1,0:T(8,128)}) custom-call(f32[8,128]{1,0:T(8,128)S(1)} %get-tuple-element.6.step_ref, f32[3,512,3072]{2,1,0:T(8,128)} %fields_ref.3, f32[3,512,3072]{2,1,0:T(8,128)} %register_ref.1, f32[512,3072]{1,0:T(8,128)} %source_ref.3, f32[1,512]{1,0:T(1,128)S(1)} %bitcast.3, ...), custom_call_target="tpu_custom_call" | custom-call | tf_op jit(solution)/shard_map/compute/pallas_call | solution.py:510
Async XLA Ops:
  0.6 26.9 %copy-start.1 = (f32[4,256,128]{2,1,0:T(8,128)S(1)}, f32[4,256,128]{2,1,0:T(8,128)}, u32[]{:S(2)}) copy-start(f32[4,256,128]{2,1,0:T(8,128)} %constant.13.clone.columns_ref) | copy-start | bytes 1572868
  0.6 26.9 %copy-start = (f32[3,256,256]{2,1,0:T(8,128)S(1)}, f32[3,256,256]{2,1,0:T(8,128)}, u32[]{:S(2)}) copy-start(f32[3,256,256]{2,1,0:T(8,128)} %constant.12.clone.maps_ref) | copy-start | bytes 2359300
  0.7 1.0 %copy-start.2 = (f32[3,112,128]{2,1,0:T(8,128)S(1)}, f32[3,112,128]{2,1,0:T(8,128)}, u32[]{:S(2)}) copy-start(f32[3,112,128]{2,1,0:T(8,128)} %constant.11.clone.lasts_ref) | copy-start | bytes 516100
  1.7 0.9 %copy-start.3 = (f32[3,112,128]{2,1,0:T(8,128)S(1)}, f32[3,112,128]{2,1,0:T(8,128)}, u32[]{:S(2)}) copy-start(f32[3,112,128]{2,1,0:T(8,128)} %constant.10.clone.firsts_ref) | copy-start | bytes 516100
  2.6 0.7 %copy-start.5 = (f32[512]{0:T(512)S(1)}, f32[512]{0:T(512)}, u32[]{:S(2)}) copy-start(f32[512]{0:T(512)} %param.13) | copy-start | bytes 6148
  3.3 24.3 %copy-start.4 = (f32[9,8,128]{2,1,0:T(8,128)S(1)}, f32[9,8,128]{2,1,0:T(8,128)}, u32[]{:S(2)}) copy-start(f32[9,8,128]{2,1,0:T(8,128)} %constant.14.clone.joins_ref) | copy-start | bytes 110596
  3.3 24.3 %copy-start.6 = (f32[512]{0:T(512)S(1)}, f32[512]{0:T(512)}, u32[]{:S(2)}) copy-start(f32[512]{0:T(512)} %param.14) | copy-start | bytes 6148

commit v2 on v1

--- a/solution.py
+++ b/solution.py
@@ -87,8 +87,10 @@
     reach = (reach_of(inv_one[:, 0]), reach_of(inv_two[:, 0]))
     columns = np.stack([inv_one[:, 0], inv_one[:, -1], inv_two[:, 0], inv_two[:, -1]])
     edge = max(reach_of(maps[k][0]) for k in range(3))
-    firsts = np.stack([maps[k][0, :edge] for k in range(3)])
-    lasts = np.stack([maps[k][-1, block - edge :] for k in range(3)])
+    weights = np.zeros((8, LANES), np.float32)
+    for k in range(3):
+        weights[k, :edge] = maps[k][0, :edge]
+        weights[3 + k, :edge] = maps[k][-1, block - edge :]
     alphas = [ALPHA_ONE] * 4 + [ALPHA_TWO] * 3
     stencils = [STENCIL_SUM] + [STENCIL_ONE] * 3 + [STENCIL_TWO] * 3
     taus = [inv_one[0, 0]] * 4 + [inv_two[0, 0]] * 3
@@ -101,7 +103,7 @@
         )
     return dict(
         maps=np.stack(maps).astype(np.float32),
-        reach=reach, columns=wide(columns), edge=edge, firsts=wide(firsts), lasts=wide(lasts),
+        reach=reach, columns=wide(columns), edge=edge, weights=weights,
         joins=wide(joins),
     )
 
@@ -132,9 +134,9 @@
 
 def talk_kernel(
     group, bundles, block, edge, chunk,
-    fields_ref, source_ref, metric_row_ref, firsts_ref, lasts_ref,
+    fields_ref, source_ref, metric_in_ref, weights_in_ref,
     halo_ref, offset_ref, step_ref,
-    metric_ref, inverse_ref, mask_ref, src, run, tops, ends, totals, total_in, edges, halo, rate, rate_in, rate_two, rate_two_in,
+    metric_row_ref, weights_row_ref, weights_ref, metric_ref, inverse_ref, mask_ref, src, run, tops, ends, totals, total_in, edges, halo, rate, rate_in, rate_two, rate_two_in,
     load_sem, tot_send, tot_recv, edge_send, edge_recv, one_send, one_recv, two_send, two_recv,
 ):
     cells, lines = src.shape
@@ -144,13 +146,15 @@
     broad = 512 if lines % 512 == 0 else chunk
 
     share = cells // LOADS
+    metric_load = pltpu.make_async_copy(metric_in_ref, metric_row_ref, load_sem.at[LOADS + 2])
+    weights_load = pltpu.make_async_copy(weights_in_ref, weights_row_ref, load_sem.at[LOADS + 3])
     loads = []
     for k in range(LOADS):
         rows = pl.ds(k * share, share)
         loads.append(pltpu.make_async_copy(source_ref.at[rows], src.at[rows], load_sem.at[k]))
     top_load = pltpu.make_async_copy(fields_ref.at[:, pl.ds(0, edge)], tops, load_sem.at[LOADS])
     end_load = pltpu.make_async_copy(fields_ref.at[:, pl.ds(cells - edge, edge)], ends, load_sem.at[LOADS + 1])
-    for load in loads + [top_load, end_load]:
+    for load in [metric_load, weights_load] + loads:
         load.start()
 
     barrier = pltpu.get_barrier_semaphore()
@@ -169,14 +173,21 @@
     def _(d):
         pl.semaphore_signal(barrier, inc=1, device_id=across(d), device_id_type=MESH)
 
+    metric_load.wait()
+    weights_load.wait()
     fill_column(metric_ref, metric_row_ref)
     fill_column(inverse_ref, metric_row_ref, lambda values: 1.0 / values)
+    for m in range(6):
+        weights_ref[m] = jnp.transpose(jnp.broadcast_to(weights_row_ref[m : m + 1], (LANES, LANES)))
     mask = lower_mask(block)
     mask_ref[:, :block] = mask
     mask_ref[:, block:] = mask
 
     for k in range(LOADS):
         loads[k].wait()
+        if k == LOADS - 2:
+            top_load.start()
+            end_load.start()
 
         @pl.loop(0, lines // broad)
         def _(j):
@@ -210,11 +221,11 @@
     @pl.loop(0, pieces)
     def _(j):
         at = pl.ds(pl.multiple_of(j * chunk, chunk), chunk)
-        for side, weights in ((0, lasts_ref), (1, firsts_ref)):
+        for side, first_weight in ((0, 3), (1, 0)):
             base = cells - edge if side == 0 else 0
             acc = jnp.zeros((8, chunk), jnp.float32)
             for r in range(0, edge, 8):
-                acc = acc + src[base + r : base + r + 8, at] * spread(weights[0, r : r + 8], chunk)
+                acc = acc + src[base + r : base + r + 8, at] * spread(weights_ref[first_weight, r : r + 8], chunk)
             edges[side, 0:1, at] = jnp.sum(acc, axis=0, keepdims=True)
             outer = cells - 1 if side == 0 else 0
             inner = cells - 2 if side == 0 else 1
@@ -226,8 +237,8 @@
                 two = jnp.zeros((8, chunk), jnp.float32)
                 for r in range(0, edge, 8):
                     value = rows[c, r : r + 8, at]
-                    one = one + value * spread(weights[1, r : r + 8], chunk)
-                    two = two + value * spread(weights[2, r : r + 8], chunk)
+                    one = one + value * spread(weights_ref[first_weight + 1, r : r + 8], chunk)
+                    two = two + value * spread(weights_ref[first_weight + 2, r : r + 8], chunk)
                 edges[side, 1 + c : 2 + c, at] = jnp.sum(one, axis=0, keepdims=True)
                 edges[side, 4 + c : 5 + c, at] = jnp.sum(two, axis=0, keepdims=True)
                 outer = edge - 1 if side == 0 else 0
@@ -242,8 +253,13 @@
         )
         for side in range(2)
     ]
-    for copy in edge_copies:
-        copy.start()
+    @pl.when(here < group - 1)
+    def _():
+        edge_copies[0].start()
+
+    @pl.when(here > 0)
+    def _():
+        edge_copies[1].start()
 
     @pl.loop(0, pieces)
     def _(j):
@@ -317,9 +333,19 @@
     step_ref[1:2, :] = jnp.where(place > 0, 1.0, 0.0)
     step_ref[2:3, :] = jnp.where(place < group - 1, 1.0, 0.0)
 
-    for copy in edge_copies:
-        copy.wait()
-    halo_ref[...] = halo[...]
+    halo_ref[...] = jnp.zeros((2, 16, lines), jnp.float32)
+
+    @pl.when(here < group - 1)
+    def _():
+        edge_copies[0].wait_send()
+        edge_copies[1].wait_recv()
+        halo_ref[1] = halo[1]
+
+    @pl.when(here > 0)
+    def _():
+        edge_copies[1].wait_send()
+        edge_copies[0].wait_recv()
+        halo_ref[0] = halo[0]
 
 
 def talk(fields, source, metric, const, group, bundles, block):
@@ -338,9 +364,10 @@
             jax.ShapeDtypeStruct((8, lines), f32),
             jax.ShapeDtypeStruct((8, LANES), f32),
         ),
-        in_specs=[held, held] + [whole] * 3,
+        in_specs=[held] * 4,
         out_specs=(whole,) * 3,
         scratch_shapes=[
+            vmem((1, cells), f32), vmem((8, LANES), f32), vmem((6, LANES, LANES), f32),
             vmem((cells, LANES), f32), vmem((cells, LANES), f32), vmem((block, 2 * block), jnp.bfloat16),
             vmem((cells, lines), f32), vmem((cells, lines), f32),
             vmem((3, edge, lines), f32), vmem((3, edge, lines), f32),
@@ -348,7 +375,7 @@
             vmem((2, 16, lines), f32), vmem((2, 16, lines), f32),
             vmem((8, LANES), f32), vmem((group, 8, LANES), f32),
             vmem((8, LANES), f32), vmem((bundles, 8, LANES), f32),
-            dma((LOADS + 2,)), dma((group,)), dma((group,)), dma((2,)), dma((2,)),
+            dma((LOADS + 4,)), dma((group,)), dma((group,)), dma((2,)), dma((2,)),
             dma((group,)), dma((group,)), dma((bundles,)), dma((bundles,)),
         ],
         compiler_params=pltpu.CompilerParams(
@@ -356,7 +383,7 @@
         ),
         name="talk",
     )(
-        fields, source, metric, jnp.asarray(const["firsts"]), jnp.asarray(const["lasts"]),
+        fields, source, metric, jnp.asarray(const["weights"]),
     )
 
 
@@ -378,8 +405,8 @@
     step_ref, fields_ref, register_ref, source_ref, metric_row_ref, curving_row_ref,
     offset_ref, halo_ref, maps_ref, columns_ref, joins_ref,
     new_fields_ref, new_register_ref, velocity_ref,
-    inverse_ref, metric_ref, curving_ref, source_map_ref, field_map_ref,
-    solved, firsts, lasts, cells_at, add,
+    inverse_ref, metric_ref, bent_ref, curving_ref, source_map_ref, field_map_ref,
+    solved, carried, squeezed, firsts, lasts, cells_at, add,
 ):
     cells, lines = source_ref.shape
     parts = cells // block
@@ -387,9 +414,11 @@
 
     @pl.when(pl.program_id(0) == 0)
     def _():
-        fill_column(metric_ref, metric_row_ref)
+        time_step = step_ref[0:1]
+        fill_column(metric_ref, metric_row_ref, lambda values: time_step * values)
+        fill_column(bent_ref, metric_row_ref, lambda values: time_step * values * values)
         fill_column(inverse_ref, metric_row_ref, lambda values: 1.0 / values)
-        fill_column(curving_ref, curving_row_ref)
+        fill_column(curving_ref, curving_row_ref, lambda values: time_step * values)
         mask = lower_mask(block)
         source_map_ref[:block, :block] = mask
         source_map_ref[:block, block : 2 * block] = mask
@@ -400,98 +429,100 @@
             table[start : start + block, block : 2 * block] = high
             table[start : start + block, 2 * block :] = low
 
+    def solve(k, c):
+        rows = slice(k * block, (k + 1) * block)
+        if c == 0:
+            value = source_ref[rows] * spread(inverse_ref[rows], lines)
+            table = source_map_ref
+        else:
+            value = fields_ref[c - 1, rows]
+            table = field_map_ref
+        high, low = two_parts(value)
+        solved[k, c] = jnp.dot(table[...], jnp.concatenate([high, low, high], axis=0), preferred_element_type=f32)
+        for s in systems[c]:
+            start = places[s][1]
+            firsts[c, k, s : s + 1] = solved[k, c, start : start + 1]
+            lasts[c, k, s : s + 1] = solved[k, c, start + block - 1 : start + block]
+            for e, r in enumerate((0, 1, block - 1, block - 2)):
+                cells_at[c, k, e, s : s + 1] = value[r : r + 1]
+
+    def far_cells(side, start):
+        own = halo_ref[side, start : start + 4]
+        return jnp.concatenate([own, own[1:4], jnp.zeros((1, lines), f32)], axis=0)
+
+    def meet(c):
+        def own(k, ends, outer, inner):
+            return ends[c, k], cells_at[c, k, outer], cells_at[c, k, inner]
+
+        _, _, near, at_edge = join(coef, halo_ref[0, 0:8], far_cells(0, 8), far_cells(0, 12), *own(0, firsts, 0, 1))
+        add[c, 0, 0], add[c, 0, 1] = near * has_before, at_edge * has_before
+        for k in range(parts - 1):
+            add[c, k, 2], add[c, k, 3], add[c, k + 1, 0], add[c, k + 1, 1] = join(
+                coef, *own(k, lasts, 2, 3), *own(k + 1, firsts, 0, 1)
+            )
+        k = parts - 1
+        near, at_edge, _, _ = join(coef, *own(k, lasts, 2, 3), halo_ref[1, 0:8], far_cells(1, 8), far_cells(1, 12))
+        add[c, k, 2], add[c, k, 3] = near * has_after, at_edge * has_after
+        if c == 0:
+            beyond = before[parts] * (1.0 - has_after)
+            add[c, k, 2, 0:1] = add[c, k, 2, 0:1] + (NEAR_ONE + FAR_ONE - FAR_ONE / ALPHA_ONE) * beyond
+            add[c, k, 3, 0:1] = add[c, k, 3, 0:1] + (FAR_ONE / ALPHA_ONE) * beyond
+        for k in range(parts):
+            for s in systems[c]:
+                start = places[s][1]
+                solved[k, c, start : start + 1] += add[c, k, 1, s : s + 1]
+                solved[k, c, start + block - 1 : start + block] += add[c, k, 3, s : s + 1]
+
+    def whole(k, c, s, r):
+        start = places[s][1]
+        kind = 0 if s < 4 else 1
+        value = solved[k, c, start + r : start + r + rows_at_once]
+        if r < reach[kind]:
+            column = spread(columns_ref[2 * kind, r : r + rows_at_once], lines)
+            value = value + column * add[c, k, 0, s : s + 1]
+        if r + rows_at_once > block - reach[kind]:
+            column = spread(columns_ref[2 * kind + 1, r : r + rows_at_once], lines)
+            value = value + column * add[c, k, 2, s : s + 1]
+        return value
+
+    def finish(k, c):
+        for r in range(0, block, rows_at_once):
+            rows = slice(k * block + r, k * block + r + rows_at_once)
+            if c == 0:
+                stretch = spread(metric_ref[rows], lines)
+                scaled = source_ref[rows] * spread(inverse_ref[rows], lines)
+                velocity = 0.5 * scaled - (before[k] + solved[k, 0, r : r + rows_at_once])
+                velocity_ref[rows] = velocity
+                carried[rows] = velocity * stretch
+                squeezed[rows] = stretch * whole(k, 0, 0, r)
+            else:
+                diffusion = DIFFUSIONS[c - 1]
+                on_slope = spread(diffusion * curving_ref[rows], lines) - carried[rows]
+                on_bend = spread(diffusion * bent_ref[rows], lines)
+                field = fields_ref[c - 1, rows]
+                change = on_slope * whole(k, c, c, r) + on_bend * whole(k, c, 3 + c, r) - field * squeezed[rows]
+                updated = KEEP_FACTOR * register_ref[c - 1, rows] + change
+                new_register_ref[c - 1, rows] = updated
+                new_fields_ref[c - 1, rows] = field + STEP_FACTOR * updated
+
+    places = [(0, block)] + [(1 + c, 0) for c in range(3)] + [(1 + c, block) for c in range(3)]
+    systems = [[s for s in range(SYSTEMS) if places[s][0] == c] for c in range(4)]
+    coef = [spread(joins_ref[i], lines) for i in range(9)]
+    has_before, has_after = spread(step_ref[1:2], lines), spread(step_ref[2:3], lines)
+
     for k in range(parts):
-        rows = slice(k * block, (k + 1) * block)
-        for c in range(4):
-            if c == 0:
-                value = source_ref[rows] * spread(inverse_ref[rows], lines)
-                table = source_map_ref
-            else:
-                value = fields_ref[c - 1, rows]
-                table = field_map_ref
-            high, low = two_parts(value)
-            solved[k, c] = jnp.dot(
-                table[...], jnp.concatenate([high, low, high], axis=0), preferred_element_type=f32
-            )
-            for e, r in enumerate((0, 1, block - 1, block - 2)):
-                row = value[r : r + 1]
-                cells_at[k, e, c : c + 1] = row
-                if c > 0:
-                    cells_at[k, e, 3 + c : 4 + c] = row
-        for into, r in ((firsts, 0), (lasts, block - 1)):
-            into[k, 0:1] = solved[k, 0, block + r : block + r + 1]
-            for c in range(3):
-                into[k, 1 + c : 2 + c] = solved[k, 1 + c, r : r + 1]
-                into[k, 4 + c : 5 + c] = solved[k, 1 + c, block + r : block + r + 1]
-            into[k, 7:8] = jnp.zeros((1, lines), f32)
-        for e in range(4):
-            cells_at[k, e, 7:8] = jnp.zeros((1, lines), f32)
-
-    coef = [spread(joins_ref[i], lines) for i in range(9)]
+        solve(k, 0)
     before = [offset_ref[0:1, :]]
     for k in range(parts):
         before.append(before[-1] + solved[k, 0, block - 1 : block])
-
-    def far_cells(side, start):
-        own = halo_ref[side, start : start + 4]
-        return jnp.concatenate([own, own[1:4], jnp.zeros((1, lines), f32)], axis=0)
-
-    has_before, has_after = spread(step_ref[1:2], lines), spread(step_ref[2:3], lines)
-    _, _, near, at_edge = join(
-        coef, halo_ref[0, 0:8], far_cells(0, 8), far_cells(0, 12), firsts[0], cells_at[0, 0], cells_at[0, 1]
-    )
-    add[0, 0], add[0, 1] = near * has_before, at_edge * has_before
-    for k in range(parts - 1):
-        add[k, 2], add[k, 3], add[k + 1, 0], add[k + 1, 1] = join(
-            coef, lasts[k], cells_at[k, 2], cells_at[k, 3],
-            firsts[k + 1], cells_at[k + 1, 0], cells_at[k + 1, 1],
-        )
-    k = parts - 1
-    near, at_edge, _, _ = join(
-        coef, lasts[k], cells_at[k, 2], cells_at[k, 3], halo_ref[1, 0:8], far_cells(1, 8), far_cells(1, 12)
-    )
-    add[k, 2], add[k, 3] = near * has_after, at_edge * has_after
-    beyond = before[parts] * (1.0 - has_after)
-    add[k, 2, 0:1] = add[k, 2, 0:1] + (NEAR_ONE + FAR_ONE - FAR_ONE / ALPHA_ONE) * beyond
-    add[k, 3, 0:1] = add[k, 3, 0:1] + (FAR_ONE / ALPHA_ONE) * beyond
-
-    time_step = spread(step_ref[0:1], lines)
+    for c in range(1, 4):
+        meet(c - 1)
+        for k in range(parts):
+            solve(k, c)
+            finish(k, c - 1)
+    meet(3)
     for k in range(parts):
-        places = [(0, block)] + [(1 + c, 0) for c in range(3)] + [(1 + c, block) for c in range(3)]
-        for s, (slot, start) in enumerate(places):
-            solved[k, slot, start : start + 1] += add[k, 1, s : s + 1]
-            solved[k, slot, start + block - 1 : start + block] += add[k, 3, s : s + 1]
-
-        for r in range(0, block, rows_at_once):
-            rows = slice(k * block + r, k * block + r + rows_at_once)
-
-            def whole(s):
-                slot, start = places[s]
-                kind = 0 if s < 4 else 1
-                value = solved[k, slot, start + r : start + r + rows_at_once]
-                if r < reach[kind]:
-                    column = spread(columns_ref[2 * kind, r : r + rows_at_once], lines)
-                    value = value + column * add[k, 0, s : s + 1]
-                if r + rows_at_once > block - reach[kind]:
-                    column = spread(columns_ref[2 * kind + 1, r : r + rows_at_once], lines)
-                    value = value + column * add[k, 2, s : s + 1]
-                return value
-
-            stretch = spread(metric_ref[rows], lines)
-            curving = spread(curving_ref[rows], lines)
-            scaled = source_ref[rows] * spread(inverse_ref[rows], lines)
-            velocity = 0.5 * scaled - (before[k] + solved[k, 0, r : r + rows_at_once])
-            velocity_ref[rows] = velocity
-            carried = velocity * stretch
-            squeezed = (time_step * stretch) * whole(0)
-            bent = time_step * stretch * stretch
-            for c in range(3):
-                on_slope = time_step * (DIFFUSIONS[c] * curving - carried)
-                field = fields_ref[c, rows]
-                change = on_slope * whole(1 + c) + (DIFFUSIONS[c] * bent) * whole(4 + c) - field * squeezed
-                updated = KEEP_FACTOR * register_ref[c, rows] + change
-                new_register_ref[c, rows] = updated
-                new_fields_ref[c, rows] = field + STEP_FACTOR * updated
+        finish(k, 3)
 
 
 def compute(fields, register, source, metric, curving, halo, offset, step, const, block):
@@ -523,13 +554,12 @@
         ],
         out_specs=(three, three, flat),
         scratch_shapes=[
-            pltpu.VMEM((cells, LANES), f32), pltpu.VMEM((cells, LANES), f32), pltpu.VMEM((cells, LANES), f32),
+            *[pltpu.VMEM((cells, LANES), f32)] * 4,
             pltpu.VMEM((2 * block, 3 * block), jnp.bfloat16), pltpu.VMEM((2 * block, 3 * block), jnp.bfloat16),
             pltpu.VMEM((parts, 4, 2 * block, width), f32),
-            pltpu.VMEM((parts, 8, width), f32),
-            pltpu.VMEM((parts, 8, width), f32),
-            pltpu.VMEM((parts, 4, 8, width), f32),
-            pltpu.VMEM((parts, 4, 8, width), f32),
+            pltpu.VMEM((cells, width), f32), pltpu.VMEM((cells, width), f32),
+            pltpu.VMEM((4, parts, 8, width), f32), pltpu.VMEM((4, parts, 8, width), f32),
+            pltpu.VMEM((4, parts, 4, 8, width), f32), pltpu.VMEM((4, parts, 4, 8, width), f32),
         ],
         compiler_params=pltpu.CompilerParams(vmem_limit_bytes=48 * 2**20),
         name="compute",

time: 67.9 us -> 68.5 us (level)
  Pallas kernels: 64.4 us -> 66.1 us
  local copies, waits for them, and re-layouts: 2.63 us -> 1.49 us
    unnamed x14 -> x12, local copies, waits for them, and re-layouts: 2.63 us -> 1.49 us
    pallas_call x1, Pallas kernels: 40.1 us -> 41.1 us  [compute(): pl.pallas_call(functools.partial(main_kernel, block, const['reach'], min(...]
    pallas_call x1, Pallas kernels: 24.2 us -> 25 us  [talk(): pl.pallas_call(functools.partial(talk_kernel, group, bundles, block, edge...]
where the time goes in v2:
time: 68.5 us; the launch traced here: 68.3 us
  Pallas kernels  66.1 us (96%)
  local copies, waits for them, and re-layouts  1.49 us (2%)
  between operations  0.7 us (1%)
    pallas_call x1, Pallas kernels, compute(): pl.pallas_call(functools.partial(main_kernel, block, const['reach'], min(...  41.1 us
    pallas_call x1, Pallas kernels, talk(): pl.pallas_call(functools.partial(talk_kernel, group, bundles, block, edge...  25 us
    unnamed x12, local copies, waits for them, and re-layouts  1.49 us

profile of v2, /device:TPU:0, one launch (start us, length us, event | category | flops | bytes accessed | tf_op | source)
XLA Modules:
  0.0 68.3 jit_solution(15594235574906407108)
XLA Ops:
  0.6 0.0 copy-start.2
  0.6 0.0 copy-start.1
  0.7 0.0 copy-start
  0.7 0.0 copy-start.3
  0.7 0.8 %copy-done.3 = f32[512]{0:T(512)S(1)} copy-done((f32[512]{0:T(512)S(1)}, f32[512]{0:T(512)}, u32[]{:S(2)}) %copy-start.3) | copy-done | bytes 2072
  1.5 0.0 copy-start.4
  1.5 0.7 %copy-done.4 = f32[8,128]{1,0:T(8,128)S(1)} copy-done((f32[8,128]{1,0:T(8,128)S(1)}, f32[8,128]{1,0:T(8,128)}, u32[]{:S(2)}) %copy-start.4) | copy-done | bytes 4120
  2.1 0.0 copy-start.5
  2.1 25.0 %talk.1 = (f32[2,16,3072]{2,1,0:T(8,128)S(1)}, f32[8,3072]{1,0:T(8,128)S(1)}, f32[8,128]{1,0:T(8,128)S(1)}) custom-call(f32[3,512,3072]{2,1,0:T(8,128)} %fields_ref.3, f32[512,3072]{1,0:T(8,128)} %source_ref.3, f32[1,512]{1,0:T(1,128)S(1)} %bitcast.2, f32[8,128]{1,0:T(8,128)S(1)} %copy-done.4), custom_call_target="tpu_custom_call" | custom-call | tf_op jit(solution)/shard_map/talk/pallas_call | solution.py:360
  27.2 0.0 copy-done.2
  27.2 0.0 copy-done.1
  27.2 0.0 copy-done
  27.2 0.0 copy-done.5
  27.2 41.1 %compute.1 = (f32[3,512,3072]{2,1,0:T(8,128)}, f32[3,512,3072]{2,1,0:T(8,128)}, f32[512,3072]{1,0:T(8,128)}) custom-call(f32[8,128]{1,0:T(8,128)S(1)} %get-tuple-element.6.step_ref, f32[3,512,3072]{2,1,0:T(8,128)} %fields_ref.3, f32[3,512,3072]{2,1,0:T(8,128)} %register_ref.1, f32[512,3072]{1,0:T(8,128)} %source_ref.3, f32[1,512]{1,0:T(1,128)S(1)} %bitcast.3, ...), custom_call_target="tpu_custom_call" | custom-call | tf_op jit(solution)/shard_map/compute/pallas_call | solution.py:541
Async XLA Ops:
  0.6 26.5 %copy-start.2 = (f32[9,8,128]{2,1,0:T(8,128)S(1)}, f32[9,8,128]{2,1,0:T(8,128)}, u32[]{:S(2)}) copy-start(f32[9,8,128]{2,1,0:T(8,128)} %constant.11.clone.joins_ref) | copy-start | bytes 110596
  0.6 26.5 %copy-start.1 = (f32[4,256,128]{2,1,0:T(8,128)S(1)}, f32[4,256,128]{2,1,0:T(8,128)}, u32[]{:S(2)}) copy-start(f32[4,256,128]{2,1,0:T(8,128)} %constant.10.clone.columns_ref) | copy-start | bytes 1572868
  0.7 26.5 %copy-start = (f32[3,256,256]{2,1,0:T(8,128)S(1)}, f32[3,256,256]{2,1,0:T(8,128)}, u32[]{:S(2)}) copy-start(f32[3,256,256]{2,1,0:T(8,128)} %constant.9.clone.maps_ref) | copy-start | bytes 2359300
  0.7 0.8 %copy-start.3 = (f32[512]{0:T(512)S(1)}, f32[512]{0:T(512)}, u32[]{:S(2)}) copy-start(f32[512]{0:T(512)} %param.12) | copy-start | bytes 6148
  1.5 0.7 %copy-start.4 = (f32[8,128]{1,0:T(8,128)S(1)}, f32[8,128]{1,0:T(8,128)}, u32[]{:S(2)}) copy-start(f32[8,128]{1,0:T(8,128)} %constant.8.clone.weights_in_ref) | copy-start | bytes 12292
  2.1 25.1 %copy-start.5 = (f32[512]{0:T(512)S(1)}, f32[512]{0:T(512)}, u32[]{:S(2)}) copy-start(f32[512]{0:T(512)} %param.13) | copy-start | bytes 6148
